TPU v7x, 32 devices: a whole 2x2x4 slice. The times are simulated.
32 devices in a mesh: groups: 2 (over y), ha: 4 (over z), ta: 2 (over x), col: 2 (over core).
Axes of the slice: x: 2, y: 2, z: 4, core: 2. Of those that a mesh axis runs over, the one named last changes fastest.
Arguments:
- tokens: bfloat16 [8, 16, 64, 768], P(('groups', 'ta'), 'ha', None, 'col'), parts along dimension 0, may hold values from -6 to 6
- norm1_gain: float32 [768], replicated, may hold values from 0.4 to 1.6
- w_qkv: bfloat16 [3, 768, 768], P(None, None, 'col'), may hold values from -0.21875 to 0.21875
- w_out: bfloat16 [768, 768], P('col'), may hold values from -0.3125 to 0.3125
- norm2_gain: float32 [768], replicated, may hold values from 0.4 to 1.6
- w_up: bfloat16 [768, 3072], P('ha', 'col'), may hold values from -0.21875 to 0.21875
- w_down: bfloat16 [3072, 768], P('col', 'ha'), may hold values from -0.109375 to 0.109375
Outputs:
- block_out: bfloat16 [8, 16, 64, 768], P(('groups', 'ta'), 'ha', None, 'col'), parts along dimension 0
There are 2 independent parts, one for each index of `groups`. A program takes and returns all parts, laid end to end along the dimension named above; an argument that names none is the same for every part. Nothing has to cross between parts.
All inputs are finite; a program needn't handle non-finite values.
Results may differ from a plain program's by a relative error of at most 0.009.
Values may be sent and summed in bfloat16 or wider, within the bound.
A program may use at most 64 MiB of HBM per device.

v0:
```python
import math
import jax
import jax.numpy as jnp
from jax import lax
from jax.sharding import PartitionSpec as P

HD = 64
EPS = 1e-05


def layer_norm(values, gain):
    mean = jnp.mean(values, -1, keepdims=True)
    centred = values - mean
    spread = jnp.mean(centred * centred, -1, keepdims=True)
    return centred * lax.rsqrt(spread + EPS) * gain


def attend(query, keys, values, dim):
    scale = 1.0 / math.sqrt(HD)
    moved_q = jnp.moveaxis(query, dim, -2)
    moved_k = jnp.moveaxis(keys, dim, -2)
    moved_v = jnp.moveaxis(values, dim, -2)
    shape = moved_q.shape
    split = shape[:-1] + (shape[-1] // HD, HD)
    scores = (
        jnp.einsum(
            "...qhd,...khd->...hqk",
            moved_q.reshape(split),
            moved_k.reshape(split),
            preferred_element_type=jnp.float32,
        )
        * scale
    )
    weights = jnp.exp(scores)
    weights = (weights / jnp.sum(weights, -1, keepdims=True)).astype(jnp.bfloat16)
    result = jnp.einsum(
        "...hqk,...khd->...qhd", weights, moved_v.reshape(split), preferred_element_type=jnp.float32
    ).astype(jnp.bfloat16)
    return jnp.moveaxis(result.reshape(shape), -2, dim)


def on_device(tokens, norm1_gain, w_qkv, w_out, norm2_gain, w_up, w_down):
    whole = lax.all_gather(tokens, "col", axis=3, tiled=True)
    frames, rows_h, width, model = whole.shape
    count = frames * rows_h * width
    half = tokens.shape[3]
    wide = whole.astype(jnp.float32).reshape(count, model)
    normed = layer_norm(wide, norm1_gain).astype(jnp.bfloat16)
    stacked = jnp.einsum("rd,sdc->src", normed, w_qkv, preferred_element_type=jnp.float32).astype(
        jnp.bfloat16
    )
    stacked = stacked.reshape(3, frames, rows_h, width, half)
    along_w = attend(stacked[0], stacked[1], stacked[2], 2)
    columns = lax.all_to_all(stacked, "ha", split_axis=3, concat_axis=2, tiled=True)
    along_h_far = attend(columns[0], columns[1], columns[2], 1)
    along_h = lax.all_to_all(along_h_far, "ha", split_axis=1, concat_axis=2, tiled=True)
    lines = lax.all_to_all(stacked, "ta", split_axis=3, concat_axis=1, tiled=True)
    along_t_far = attend(lines[0], lines[1], lines[2], 0)
    along_t = lax.all_to_all(along_t_far, "ta", split_axis=0, concat_axis=2, tiled=True)
    mixed = (
        along_w.astype(jnp.float32) + along_h.astype(jnp.float32) + along_t.astype(jnp.float32)
    ).astype(jnp.bfloat16)
    terms = jnp.dot(mixed.reshape(count, half), w_out, preferred_element_type=jnp.float32)
    offset = lax.axis_index("col") * half
    summed = lax.psum(terms, "col")
    first_full = wide + summed
    second = layer_norm(first_full, norm2_gain).astype(jnp.bfloat16)
    first = lax.dynamic_slice_in_dim(first_full, offset, half, 1)
    upper = jnp.dot(
        second, lax.all_gather(w_up, "ha", axis=0, tiled=True), preferred_element_type=jnp.float32
    )
    hidden = jax.nn.gelu(upper, approximate=False).astype(jnp.bfloat16)
    down_terms = jnp.dot(
        hidden, lax.all_gather(w_down, "ha", axis=1, tiled=True), preferred_element_type=jnp.float32
    )
    down_share = lax.psum_scatter(
        down_terms.astype(jnp.bfloat16), "col", scatter_dimension=1, tiled=True
    ).astype(jnp.float32)
    return (first + down_share).astype(jnp.bfloat16).reshape(frames, rows_h, width, half)


def solution(mesh):
    placed = (
        P(("groups", "ta"), "ha", None, "col"),
        P(),
        P(None, None, "col"),
        P("col", None),
        P(),
        P("ha", "col"),
        P("col", "ha"),
    )
    return jax.shard_map(
        on_device,
        mesh=mesh,
        in_specs=placed,
        out_specs=P(("groups", "ta"), "ha", None, "col"),
        check_vma=False,
    )
```

profile of v0, /device:TPU:0, one launch (start us, length us, event | category | flops | bytes accessed | tf_op | source)
XLA Modules:
  0.0 270.8 jit_solution(178408443112723178)
XLA Ops:
  7.4 2.8 %all_gather.9 = bf16[2,4,64,768]{3,2,1,0:T(8,128)(2,1)S(1)} all-gather(bf16[2,4,64,384]{3,2,1,0:T(8,128)(2,1)} %param.7), channel_id=1, replica_groups=mesh['groups'=2,'ha'=4,'ta'=2,'col'=2] {'col'}, dimensions={3}, use_global_device_ids=true | all-gather | bytes 1179648 | tf_op jit(solution)/shard_map/all_gather | solution.py:43
  10.3 0.3 fusion.11
  11.2 1.2 convolution_convert_fusion
  12.4 1.0 copy-done.4
  13.4 0.9 copy.127
  14.4 1.0 copy-done.1
  15.4 19.9 %all_to_all.48 = bf16[3,2,4,64,384]{4,2,1,0,3:T(4,128)(2,1)} all-to-all(bf16[3,2,4,64,384]{4,2,1,0,3:T(4,128)(2,1)S(1)} %copy.127), channel_id=1, replica_groups=mesh['groups'=2,'ha'=4,'ta'=2,'col'=2] {'ta'}, dimensions={3} | all-to-all | bytes 2359296 | tf_op jit(solution)/shard_map/all_to_all | solution.py:57
  35.3 5.1 %all-to-all-start = ((bf16[3,2,4,64,384]{4,2,1,0,3:T(4,128)(2,1)}), bf16[3,2,4,64,384]{4,2,1,0,3:T(4,128)(2,1)}, u32[]{:S(2)}, u32[]{:S(2)}) async-start(bf16[3,2,4,64,384]{4,2,1,0,3:T(4,128)(2,1)} %copy-done.1), calls=%async_computation | async-start | bytes 2359296 | tf_op jit(solution)/shard_map/all_to_all | solution.py:54
  40.4 2.1 fusion.92
  42.5 2.4 reshape.133
  44.9 1.5 reshape.134
  46.5 1.5 copy.145
  47.9 0.9 fusion.93
  48.8 0.8 copy.148
  49.6 2.4 reshape.139
  52.0 1.8 copy.150
  53.8 2.4 reshape.140
  56.2 3.9 %fusion.23 = f32[4,32,6,4,4]{3,4,2,1,0:T(4,128)} fusion(bf16[4,32,4,6,64]{4,3,1,0,2:T(8,128)(2,1)} %reshape.140, bf16[4,32,4,6,64]{4,3,1,0,2:T(8,128)(2,1)} %reshape.139), kind=kOutput, calls=%fused_computation.46 | convolution fusion | flops 1572864 | bytes 835584 | tf_op jit(solution)/shard_map/...qhd,...khd->...hqk/dot_general | solution.py:26
  60.1 1.9 copy.154
  62.1 0.8 divide_convert_fusion.4
  62.9 2.3 copy.156
  65.2 0.8 copy.146
  66.0 2.4 reshape.138
  68.4 2.4 fusion.21
  70.8 1.2 copy.157
  72.0 1.9 reshape.124
  73.9 0.8 copy.158
  74.7 4.4 %all-to-all-start.3 = ((bf16[4,4,32,384]{3,2,1,0:T(8,128)(2,1)}), bf16[4,4,32,384]{3,2,1,0:T(8,128)(2,1)}, u32[]{:S(2)}, u32[]{:S(2)}) async-start(bf16[4,4,32,384]{3,2,1,0:T(8,128)(2,1)} %copy.158), calls=%async_computation.3 | async-start | bytes 786432 | tf_op jit(solution)/shard_map/all_to_all | solution.py:59
  79.1 1.5 copy.128
  80.5 0.9 fusion.91
  81.4 0.8 copy.131
  82.2 2.4 reshape.136
  84.6 1.8 copy.133
  86.4 2.4 reshape.137
  88.8 0.8 copy.129
  89.6 2.4 reshape.135
  92.1 3.8 %multiply_exponential_fusion = f32[2,16,6,16,16]{3,4,2,1,0:T(8,128)} fusion(bf16[2,16,16,6,64]{4,3,1,2,0:T(8,128)(2,1)} %reshape.137, bf16[2,16,16,6,64]{4,3,1,2,0:T(8,128)(2,1)} %reshape.136), kind=kOutput, calls=%fused_computation.32 | convolution fusion | flops 6340608 | bytes 983040 | tf_op jit(solution)/shard_map/...qhd,...khd->...hqk/dot_general | solution.py:26
  95.9 3.9 %fusion.20 = bf16[2,16,16,6,64]{4,2,3,1,0:T(8,128)(2,1)} fusion(f32[2,16,6,16,16]{3,4,2,1,0:T(8,128)} %multiply_exponential_fusion, bf16[2,16,16,6,64]{4,3,1,2,0:T(8,128)(2,1)} %reshape.135), kind=kOutput, calls=%fused_computation.41 | convolution fusion | flops 6589455 | bytes 983040 | tf_op jit(solution)/shard_map/...hqk,...khd->...qhd/dot_general | solution.py:36
  99.8 2.4 copy.139
  102.2 1.9 reshape.120
  104.0 0.8 copy.140
  104.9 5.1 %all-to-all-start.1 = ((bf16[2,16,16,384]{3,2,0,1:T(8,128)(2,1)}), bf16[2,16,16,384]{3,2,0,1:T(8,128)(2,1)}, u32[]{:S(2)}, u32[]{:S(2)}) async-start(bf16[2,16,16,384]{3,2,0,1:T(8,128)(2,1)} %copy.140), calls=%async_computation.1 | async-start | bytes 786432 | tf_op jit(solution)/shard_map/all_to_all | solution.py:56
  110.0 3.3 %multiply_exponential_fusion.1 = f32[2,4,6,64,64]{3,4,2,1,0:T(8,128)} fusion(bf16[2,4,64,6,64]{4,3,2,1,0:T(8,128)(2,1)} %reshape.134, bf16[2,4,64,6,64]{4,3,2,1,0:T(8,128)(2,1)} %reshape.133), kind=kOutput, calls=%fused_computation.34 | convolution fusion | flops 25362432 | bytes 1572864 | tf_op jit(solution)/shard_map/...qhd,...khd->...hqk/dot_general | solution.py:26
  113.2 1.5 reshape.132
  114.8 3.8 %convert_bitcast_fusion = f32[2,4,64,6,64]{2,4,3,1,0:T(8,128)} fusion(f32[2,4,6,64,64]{3,4,2,1,0:T(8,128)} %multiply_exponential_fusion.1, bf16[2,4,64,6,64]{4,3,2,1,0:T(8,128)(2,1)} %reshape.132), kind=kOutput, calls=%fused_computation.28 | convolution fusion | flops 25955392 | bytes 1966080 | tf_op jit(solution)/shard_map/...hqk,...khd->...qhd/dot_general | solution.py:36
  118.6 3.6 %copy.126 = f32[2,4,64,6,64]{2,1,0,4,3:T(4,128)} copy(f32[2,4,64,6,64]{2,4,3,1,0:T(8,128)} %convert_bitcast_fusion) | data formatting | bytes 1572864 | tf_op jit(solution)/shard_map/convert_element_type | solution.py:61
  122.2 3.1 %reshape.126 = f32[512,384]{0,1:T(8,128)} reshape(f32[2,4,64,6,64]{2,1,0,4,3:T(4,128)} %copy.126) | data formatting | bytes 1572864 | tf_op jit(solution)/shard_map/convert_element_type | solution.py:61
  125.4 1.1 convert_bitcast_fusion.1
  126.5 1.2 copy.160
  127.7 1.0 copy.141
  128.9 1.2 copy.143
  130.0 3.6 %fusion.44 = f32[512,768]{1,0:T(8,128)} fusion(bf16[384,768]{1,0:T(8,128)(2,1)} %param.10, f32[512,384]{0,1:T(8,128)} %copy.160, f32[512,384]{0,1:T(8,128)} %reshape.126, f32[512,384]{0,1:T(8,128)} %copy.143), kind=kOutput, calls=%fused_computation.64 | convolution fusion | flops 302579712 | bytes 4521984 | tf_op jit(solution)/shard_map/dot_general | solution.py:63
  133.7 0.5 all-gather.3.cloned.1.call-update
  134.3 0.5 all-gather.5.cloned.1.call-update
  135.1 20.9 %all-reduce.2.cloned.1.call-done = f32[512,768]{1,0:T(8,128)} async-done(((f32[512,768]{1,0:T(8,128)}), f32[512,768]{1,0:T(8,128)}) %all-reduce.2.cloned.1.call-update) | async-done | bytes 1572880 | tf_op jit(solution)/shard_map/psum | solution.py:65
  156.0 1.6 fusion.90
  157.7 1.1 copy-done.2
  159.1 28.4 %all-gather.3.cloned.1.call-done = bf16[768,1536]{1,0:T(8,128)(2,1)} async-done(((bf16[192,1536]{1,0:T(8,128)(2,1)}), bf16[768,1536]{1,0:T(8,128)(2,1)}) %all-gather.3.cloned.1.call-update) | async-done | bytes 2359312 | tf_op jit(solution)/shard_map/all_gather | solution.py:70
  187.6 50.3 %all-gather.5.cloned.1.call-done = bf16[1536,768]{0,1:T(8,128)(2,1)} async-done(((bf16[1536,192]{0,1:T(8,128)(2,1)}), bf16[1536,768]{0,1:T(8,128)(2,1)}) %all-gather.5.cloned.1.call-update) | async-done | bytes 2359312 | tf_op jit(solution)/shard_map/all_gather | solution.py:74
  237.8 12.3 %fusion.17 = bf16[512,768]{1,0:T(8,128)(2,1)} fusion(bf16[1536,768]{0,1:T(8,128)(2,1)} %all-gather.5.cloned.1.call-done, bf16[768,1536]{1,0:T(8,128)(2,1)} %all-gather.3.cloned.1.call-done, f32[512,768]{1,0:T(8,128)} %copy-done.2, f32[768]{0:T(1024)S(1)} %copy-done.6, f32[512]{0:T(512)S(1)} %add_rsqrt_fusion.1, f32[512]{0:T(512)S(1)} %broadcast_multiply_fusion.1), kind=kOutput, calls=%fused_computation.37 | convolution fusion | flops 2469003264 | bytes 7085056 | tf_op jit(solution)/shard_map/dot_general | solution.py:73
  250.1 2.4 copy.181
  252.6 7.0 %reduce-scatter.4.cloned.1.call-done = bf16[384,512]{1,0:T(8,128)(2,1)} async-done(((bf16[768,512]{1,0:T(8,128)(2,1)}), bf16[384,512]{1,0:T(8,128)(2,1)}) %reduce-scatter.4.cloned.1.call-update) | async-done | bytes 393232
  259.6 1.9 copy.182
  261.5 1.8 add_convert_fusion
  (33 shorter events, 1.8 us)
Async XLA Ops:
  7.4 3.8 %copy-start = (bf16[3,768,384]{2,1,0:T(8,128)(2,1)S(1)}, bf16[3,768,384]{2,1,0:T(8,128)(2,1)}, u32[]{:S(2)}) copy-start(bf16[3,768,384]{2,1,0:T(8,128)(2,1)} %param.9) | copy-start | bytes 5308420
  7.4 3.5 %copy-start.5 = (f32[768]{0:T(1024)S(1)}, f32[768]{0:T(1024)}, u32[]{:S(2)}) copy-start(f32[768]{0:T(1024)} %param.8) | copy-start | bytes 9220
  12.4 1.0 copy-start.4
  14.4 1.0 copy-start.1
  35.3 39.4 %all-to-all-start = ((bf16[3,2,4,64,384]{4,2,1,0,3:T(4,128)(2,1)}), bf16[3,2,4,64,384]{4,2,1,0,3:T(4,128)(2,1)}, u32[]{:S(2)}, u32[]{:S(2)}) async-start(bf16[3,2,4,64,384]{4,2,1,0,3:T(4,128)(2,1)} %copy-done.1), calls=%async_computation | async-start | bytes 2359296 | tf_op jit(solution)/shard_map/all_to_all | solution.py:54
  74.7 30.2 %all-to-all-start.3 = ((bf16[4,4,32,384]{3,2,1,0:T(8,128)(2,1)}), bf16[4,4,32,384]{3,2,1,0:T(8,128)(2,1)}, u32[]{:S(2)}, u32[]{:S(2)}) async-start(bf16[4,4,32,384]{3,2,1,0:T(8,128)(2,1)} %copy.158), calls=%async_computation.3 | async-start | bytes 786432 | tf_op jit(solution)/shard_map/all_to_all | solution.py:59
  104.9 22.8 %all-to-all-start.1 = ((bf16[2,16,16,384]{3,2,0,1:T(8,128)(2,1)}), bf16[2,16,16,384]{3,2,0,1:T(8,128)(2,1)}, u32[]{:S(2)}, u32[]{:S(2)}) async-start(bf16[2,16,16,384]{3,2,0,1:T(8,128)(2,1)} %copy.140), calls=%async_computation.1 | async-start | bytes 786432 | tf_op jit(solution)/shard_map/all_to_all | solution.py:56
  110.0 46.1 %all-reduce.2.cloned.1.call-start = ((), (), s32[]{:S(2)}) async-start(), calls=%async_computation.5 | async-start | bytes 3145728 | tf_op jit(solution)/shard_map/psum | solution.py:65
  133.7 53.9 %all-gather.3.cloned.1.call-start = ((), (), s32[]{:S(2)}) async-start(), calls=%async_computation.6 | async-start | bytes 2949120 | tf_op jit(solution)/shard_map/all_gather | solution.py:70
  134.2 103.6 %all-gather.5.cloned.1.call-start = ((), (), s32[]{:S(2)}) async-start(), calls=%async_computation.7 | async-start | bytes 2949120 | tf_op jit(solution)/shard_map/all_gather | solution.py:74
  134.8 103.0 %copy-start.6 = (f32[768]{0:T(1024)S(1)}, f32[768]{0:T(1024)}, u32[]{:S(2)}) copy-start(f32[768]{0:T(1024)} %param.11) | copy-start | bytes 9220
  134.8 124.8 %reduce-scatter.4.cloned.1.call-start = ((), (), s32[]{:S(2)}) async-start(), calls=%async_computation.8 | async-start | bytes 1179648
  157.7 1.2 copy-start.2
  250.1 11.4 %copy-start.3 = (f32[512,768]{1,0:T(8,128)S(1)}, f32[512,768]{1,0:T(8,128)}, u32[]{:S(2)}) copy-start(f32[512,768]{1,0:T(8,128)} %copy-done.2) | copy-start | bytes 4718596
Sparse Core Ops, SparseCore 0:
  133.8 22.2 all-reduce.1
  252.7 6.8 reduce-scatter.3
Sparse Core Ops, SparseCore 1:
  135.8 51.7 all-gather.2
  189.1 48.7 all-gather.4
where the time goes:
time: 272 us; the launch traced here: 271 us
  waiting for transfers between devices  108 us (40%)
  local copies, waits for them, and re-layouts  65.5 us (24%)
  matrix products  38.2 us (14%)
  blocking collectives  22.7 us (8%)
  between operations  15 us (6%)
  starting transfers between devices  14.9 us (5%)
  other arithmetic  6.71 us (2%)
    all_gather x1, waiting for transfers between devices, on_device(): lax.all_gather(w_down, 'ha', axis=1, tiled=True)  50.3 us
    all_gather x1, waiting for transfers between devices, on_device(): lax.all_gather(w_up, 'ha', axis=0, tiled=True)  28.4 us
    psum x1, waiting for transfers between devices, on_device(): summed = lax.psum(terms, 'col')  20.9 us
    all_to_all x1, blocking collectives, on_device(): lax.all_to_all(stacked, 'ta', split_axis=3, concat_axis=1, tiled=True)  19.9 us
    dot_general x1, matrix products, on_device(): jnp.dot(hidden, lax.all_gather(w_down, 'ha', axis=1, tiled=True), preferr...  12.3 us
    dot_general x3, matrix products, attend(): jnp.einsum('...qhd,...khd->...hqk', moved_q.reshape(split), moved_k.resha...  10.9 us
    dot_general x3, matrix products, attend(): jnp.einsum('...hqk,...khd->...qhd', weights, moved_v.reshape(split), pref...  10.2 us
    unnamed x5, waiting for transfers between devices  8.13 us
  transfers between devices with their start and end apart: 7, of which 4 were waited for; matrix products, arithmetic and copies ran while one was open for 29% of the time, Pallas kernels for 0%

commit v1 on v0

--- a/solution.py
+++ b/solution.py
@@ -6,6 +6,17 @@
 
 HD = 64
 EPS = 1e-05
+
+
+def cut_along(x, dim, peers):
+    before, after = (x.shape[:dim], x.shape[dim + 1 :])
+    return jnp.moveaxis(x.reshape(*before, peers, -1, *after), dim, 0)
+
+
+def joined_along(blocks, dim):
+    blocks = jnp.moveaxis(blocks, 0, dim)
+    lengths = blocks.shape
+    return blocks.reshape(*lengths[:dim], lengths[dim] * lengths[dim + 1], *lengths[dim + 2 :])
 
 
 def layer_norm(values, gain):
@@ -53,7 +64,14 @@
     along_w = attend(stacked[0], stacked[1], stacked[2], 2)
     columns = lax.all_to_all(stacked, "ha", split_axis=3, concat_axis=2, tiled=True)
     along_h_far = attend(columns[0], columns[1], columns[2], 1)
-    along_h = lax.all_to_all(along_h_far, "ha", split_axis=1, concat_axis=2, tiled=True)
+    size, mine = (lax.axis_size("ha"), lax.axis_index("ha"))
+    pieces = cut_along(along_h_far, 1, size)
+    finished = [pieces[mine]]
+    for lap in range(1, size):
+        sent = pieces[mine ^ lap]
+        finished.append(lax.ppermute(sent, "ha", [(i, i ^ lap) for i in range(size)]))
+    pieces = jnp.stack(finished)[mine ^ jnp.arange(size)]
+    along_h = joined_along(pieces, 2)
     lines = lax.all_to_all(stacked, "ta", split_axis=3, concat_axis=1, tiled=True)
     along_t_far = attend(lines[0], lines[1], lines[2], 0)
     along_t = lax.all_to_all(along_t_far, "ta", split_axis=0, concat_axis=2, tiled=True)

time: 272 us -> 258 us (0.949)
  blocking collectives: 22.7 us -> 2.78 us
  waiting for transfers between devices: 108 us -> 121 us
  local copies, waits for them, and re-layouts: 65.5 us -> 55.7 us
  starting transfers between devices: 14.9 us -> 18.8 us
    all_to_all x1 -> x0, blocking collectives: 19.9 us -> none  [on_device(): lax.all_to_all(stacked, 'ta', split_axis=3, concat_axis=1, tiled=True)]
    all_to_all x1, waiting for transfers between devices: 0.01 us -> 10.8 us  [on_device(): lax.all_to_all(stacked, 'ta', split_axis=3, concat_axis=1, tiled=True)]
    ppermute x0 -> x3, waiting for transfers between devices: none -> 4.5 us  [on_device(): lax.ppermute(sent, 'ha', [(i, i ^ lap) for i in range(size)])]
    ppermute x0 -> x3, starting transfers between devices: none -> 4.39 us  [on_device(): lax.ppermute(sent, 'ha', [(i, i ^ lap) for i in range(size)])]
  transfers between devices with their start and end apart: 7 -> 10, of which waited for: 4 -> 7; matrix products, arithmetic and copies ran while one was open for 29% -> 27% of each run, Pallas kernels for 0% -> 0%
where the time goes in v1:
time: 258 us; the launch traced here: 257 us
  waiting for transfers between devices  121 us (47%)
  local copies, waits for them, and re-layouts  55.7 us (22%)
  matrix products  36.4 us (14%)
  starting transfers between devices  18.8 us (7%)
  between operations  15.1 us (6%)
  other arithmetic  7.22 us (3%)
  blocking collectives  2.78 us (1%)
    all_gather x1, waiting for transfers between devices, on_device(): lax.all_gather(w_down, 'ha', axis=1, tiled=True)  50.2 us
    all_gather x1, waiting for transfers between devices, on_device(): lax.all_gather(w_up, 'ha', axis=0, tiled=True)  28.5 us
    psum x1, waiting for transfers between devices, on_device(): summed = lax.psum(terms, 'col')  19 us
    dot_general x1, matrix products, on_device(): jnp.dot(hidden, lax.all_gather(w_down, 'ha', axis=1, tiled=True), preferr...  11.4 us
    dot_general x3, matrix products, attend(): jnp.einsum('...qhd,...khd->...hqk', moved_q.reshape(split), moved_k.resha...  10.9 us
    all_to_all x1, waiting for transfers between devices, on_device(): lax.all_to_all(stacked, 'ta', split_axis=3, concat_axis=1, tiled=True)  10.8 us
    dot_general x3, matrix products, attend(): jnp.einsum('...hqk,...khd->...qhd', weights, moved_v.reshape(split), pref...  9.26 us
    unnamed x5, waiting for transfers between devices  8.13 us
  transfers between devices with their start and end apart: 10, of which 7 were waited for; matrix products, arithmetic and copies ran while one was open for 27% of the time, Pallas kernels for 0%

profile of v1, /device:TPU:0, one launch (start us, length us, event | category | flops | bytes accessed | tf_op | source)
XLA Modules:
  0.0 257.1 jit_solution(10478982688695002575)
XLA Ops:
  7.4 2.8 %all_gather.9 = bf16[2,4,64,768]{3,2,1,0:T(8,128)(2,1)S(1)} all-gather(bf16[2,4,64,384]{3,2,1,0:T(8,128)(2,1)} %param.7), channel_id=1, replica_groups=mesh['groups'=2,'ha'=4,'ta'=2,'col'=2] {'col'}, dimensions={3}, use_global_device_ids=true | all-gather | bytes 1179648 | tf_op jit(solution)/shard_map/all_gather | solution.py:54
  11.2 1.2 convolution_convert_fusion
  12.4 1.0 copy-done.2
  13.4 1.9 copy.134
  15.4 4.5 %all-to-all-start.1 = ((bf16[3,2,4,64,384]{4,2,1,0,3:T(4,128)(2,1)}), bf16[3,2,4,64,384]{4,2,1,0,3:T(4,128)(2,1)}, u32[]{:S(2)}, u32[]{:S(2)}) async-start(bf16[3,2,4,64,384]{4,2,1,0,3:T(4,128)(2,1)} %copy.134), calls=%async_computation.1 | async-start | bytes 2359296 | tf_op jit(solution)/shard_map/all_to_all | solution.py:75
  19.9 2.1 fusion.93
  22.0 2.4 reshape.166
  24.3 1.5 reshape.167
  25.9 10.8 %all-to-all-done.1 = bf16[3,2,4,64,384]{4,2,1,0,3:T(4,128)(2,1)} async-done(((bf16[3,2,4,64,384]{4,2,1,0,3:T(4,128)(2,1)}), bf16[3,2,4,64,384]{4,2,1,0,3:T(4,128)(2,1)}, u32[]{:S(2)}, u32[]{:S(2)}) %all-to-all-start.1) | async-done | bytes 1179680 | tf_op jit(solution)/shard_map/all_to_all | solution.py:75
  36.6 5.1 %all-to-all-start = ((bf16[3,2,4,64,384]{4,2,1,0,3:T(4,128)(2,1)}), bf16[3,2,4,64,384]{4,2,1,0,3:T(4,128)(2,1)}, u32[]{:S(2)}, u32[]{:S(2)}) async-start(bf16[3,2,4,64,384]{4,2,1,0,3:T(4,128)(2,1)} %copy.134), calls=%async_computation | async-start | bytes 2359296 | tf_op jit(solution)/shard_map/all_to_all | solution.py:65
  41.8 3.3 %multiply_exponential_fusion.1 = f32[2,4,6,64,64]{3,4,2,1,0:T(8,128)} fusion(bf16[2,4,64,6,64]{4,3,2,1,0:T(8,128)(2,1)} %reshape.167, bf16[2,4,64,6,64]{4,3,2,1,0:T(8,128)(2,1)} %reshape.166), kind=kOutput, calls=%fused_computation.35 | convolution fusion | flops 25362432 | bytes 1572864 | tf_op jit(solution)/shard_map/...qhd,...khd->...hqk/dot_general | solution.py:37
  45.0 1.5 reshape.165
  46.5 3.8 %convert_bitcast_fusion = f32[2,4,64,6,64]{2,4,3,1,0:T(8,128)} fusion(f32[2,4,6,64,64]{3,4,2,1,0:T(8,128)} %multiply_exponential_fusion.1, bf16[2,4,64,6,64]{4,3,2,1,0:T(8,128)(2,1)} %reshape.165), kind=kOutput, calls=%fused_computation.29 | convolution fusion | flops 25955392 | bytes 1966080 | tf_op jit(solution)/shard_map/...hqk,...khd->...qhd/dot_general | solution.py:47
  50.4 3.6 %copy.133 = f32[2,4,64,6,64]{2,1,0,4,3:T(4,128)} copy(f32[2,4,64,6,64]{2,4,3,1,0:T(8,128)} %convert_bitcast_fusion) | data formatting | bytes 1572864 | tf_op jit(solution)/shard_map/convert_element_type | solution.py:79
  54.0 3.1 %reshape.152 = f32[512,384]{0,1:T(8,128)} reshape(f32[2,4,64,6,64]{2,1,0,4,3:T(4,128)} %copy.133) | data formatting | bytes 1572864 | tf_op jit(solution)/shard_map/convert_element_type | solution.py:79
  57.1 1.5 copy.154
  58.7 0.8 copy.157
  59.5 2.4 reshape.172
  62.0 0.8 copy.159
  62.8 2.4 reshape.173
  65.1 3.8 %fusion.23 = f32[4,32,6,4,4]{3,4,2,1,0:T(4,128)} fusion(bf16[4,32,4,6,64]{4,3,1,0,2:T(8,128)(2,1)} %reshape.173, bf16[4,32,4,6,64]{4,3,1,0,2:T(8,128)(2,1)} %reshape.172), kind=kOutput, calls=%fused_computation.46 | convolution fusion | flops 1572864 | bytes 835584 | tf_op jit(solution)/shard_map/...qhd,...khd->...hqk/dot_general | solution.py:37
  69.0 1.9 copy.163
  71.1 1.6 copy.165
  72.8 1.5 reshape.171
  74.3 2.4 fusion.21
  76.7 1.2 copy.166
  77.9 1.9 reshape.150
  79.7 0.8 copy.167
  80.5 4.2 %all-to-all-start.2 = ((bf16[4,4,32,384]{3,2,1,0:T(8,128)(2,1)}), bf16[4,4,32,384]{3,2,1,0:T(8,128)(2,1)}, u32[]{:S(2)}, u32[]{:S(2)}) async-start(bf16[4,4,32,384]{3,2,1,0:T(8,128)(2,1)} %copy.167), calls=%async_computation.2 | async-start | bytes 786432 | tf_op jit(solution)/shard_map/all_to_all | solution.py:77
  85.0 1.5 copy.135
  86.6 0.8 copy.138
  87.4 2.4 reshape.169
  89.8 0.8 copy.140
  90.6 2.4 reshape.170
  93.0 1.5 reshape.168
  94.5 3.8 %multiply_exponential_fusion = f32[2,16,6,16,16]{3,4,2,1,0:T(8,128)} fusion(bf16[2,16,16,6,64]{4,3,1,2,0:T(8,128)(2,1)} %reshape.170, bf16[2,16,16,6,64]{4,3,1,2,0:T(8,128)(2,1)} %reshape.169), kind=kOutput, calls=%fused_computation.33 | convolution fusion | flops 6340608 | bytes 983040 | tf_op jit(solution)/shard_map/...qhd,...khd->...hqk/dot_general | solution.py:37
  98.4 3.0 %fusion.20 = bf16[2,16,16,6,64]{4,2,3,1,0:T(8,128)(2,1)S(1)} fusion(f32[2,16,6,16,16]{3,4,2,1,0:T(8,128)} %multiply_exponential_fusion, bf16[2,16,16,6,64]{4,3,1,2,0:T(8,128)(2,1)} %reshape.168), kind=kOutput, calls=%fused_computation.42 | convolution fusion | flops 6589455 | bytes 983040 | tf_op jit(solution)/shard_map/...hqk,...khd->...qhd/dot_general | solution.py:47
  101.4 1.2 copy.146
  102.6 1.9 reshape.145
  104.7 0.6 copy.228
  105.4 2.0 collective-permute-start
  107.4 0.7 copy.227
  108.1 2.4 collective-permute-start.1
  110.4 0.7 copy.226
  111.1 1.1 convert_bitcast_fusion.1
  112.2 1.2 copy.169
  113.4 3.2 %collective-permute-done.1 = bf16[2,4,16,384]{3,2,1,0:T(8,128)(2,1)} collective-permute-done((bf16[2,4,16,384]{3,2,1,0:T(8,128)(2,1)}, bf16[2,4,16,384]{3,2,1,0:T(8,128)(2,1)}, u32[]{:S(2)}, u32[]{:S(2)}) %collective-permute-start.1) | collective-permute-done | bytes 98336 | tf_op jit(solution)/shard_map/ppermute | solution.py:72
  116.7 1.3 collective-permute-done.2
  117.9 1.0 pad_maximum_fusion
  118.9 0.6 gather_fusion
  119.7 1.2 copy.152
  120.9 3.6 %fusion.44 = f32[512,768]{1,0:T(8,128)} fusion(bf16[384,768]{1,0:T(8,128)(2,1)} %param.10, f32[512,384]{0,1:T(8,128)} %copy.169, f32[512,384]{0,1:T(8,128)} %reshape.152, f32[512,384]{0,1:T(8,128)} %copy.152), kind=kOutput, calls=%fused_computation.65 | convolution fusion | flops 302579712 | bytes 4521984 | tf_op jit(solution)/shard_map/dot_general | solution.py:81
  124.6 0.5 all-gather.3.cloned.1.call-update
  125.2 0.5 all-gather.5.cloned.1.call-update
  126.0 19.0 %all-reduce.2.cloned.1.call-done = f32[512,768]{1,0:T(8,128)} async-done(((f32[512,768]{1,0:T(8,128)}), f32[512,768]{1,0:T(8,128)}) %all-reduce.2.cloned.1.call-update) | async-done | bytes 1572880 | tf_op jit(solution)/shard_map/psum | solution.py:83
  145.0 1.6 fusion.91
  146.7 1.2 copy-done.1
  148.1 28.5 %all-gather.3.cloned.1.call-done = bf16[768,1536]{1,0:T(8,128)(2,1)} async-done(((bf16[192,1536]{1,0:T(8,128)(2,1)}), bf16[768,1536]{1,0:T(8,128)(2,1)}) %all-gather.3.cloned.1.call-update) | async-done | bytes 2359312 | tf_op jit(solution)/shard_map/all_gather | solution.py:88
  176.6 50.2 %all-gather.5.cloned.1.call-done = bf16[1536,768]{0,1:T(8,128)(2,1)} async-done(((bf16[1536,192]{0,1:T(8,128)(2,1)}), bf16[1536,768]{0,1:T(8,128)(2,1)}) %all-gather.5.cloned.1.call-update) | async-done | bytes 2359312 | tf_op jit(solution)/shard_map/all_gather | solution.py:92
  226.8 11.4 %fusion.17 = bf16[512,768]{1,0:T(8,128)(2,1)S(1)} fusion(bf16[1536,768]{0,1:T(8,128)(2,1)} %all-gather.5.cloned.1.call-done, bf16[768,1536]{1,0:T(8,128)(2,1)} %all-gather.3.cloned.1.call-done, f32[512,768]{1,0:T(8,128)} %copy-done.1, f32[768]{0:T(1024)S(1)} %copy-done.4, f32[512]{0:T(512)S(1)} %add_rsqrt_fusion.1, f32[512]{0:T(512)S(1)} %broadcast_multiply_fusion.1), kind=kOutput, calls=%fused_computation.38 | convolution fusion | flops 2469003264 | bytes 7085056 | tf_op jit(solution)/shard_map/dot_general | solution.py:91
  238.2 1.2 copy.190
  239.4 7.0 %reduce-scatter.4.cloned.1.call-done = bf16[384,512]{1,0:T(8,128)(2,1)} async-done(((bf16[768,512]{1,0:T(8,128)(2,1)}), bf16[384,512]{1,0:T(8,128)(2,1)}) %reduce-scatter.4.cloned.1.call-update) | async-done | bytes 393232
  246.5 1.2 copy.191
  247.7 2.0 add_convert_fusion
  (42 shorter events, 3.2 us)
Async XLA Ops:
  7.4 3.8 %copy-start = (bf16[3,768,384]{2,1,0:T(8,128)(2,1)S(1)}, bf16[3,768,384]{2,1,0:T(8,128)(2,1)}, u32[]{:S(2)}) copy-start(bf16[3,768,384]{2,1,0:T(8,128)(2,1)} %param.9) | copy-start | bytes 5308420
  7.4 3.5 %copy-start.3 = (f32[768]{0:T(1024)S(1)}, f32[768]{0:T(1024)}, u32[]{:S(2)}) copy-start(f32[768]{0:T(1024)} %param.8) | copy-start | bytes 9220
  12.4 1.0 copy-start.2
  15.4 21.3 %all-to-all-start.1 = ((bf16[3,2,4,64,384]{4,2,1,0,3:T(4,128)(2,1)}), bf16[3,2,4,64,384]{4,2,1,0,3:T(4,128)(2,1)}, u32[]{:S(2)}, u32[]{:S(2)}) async-start(bf16[3,2,4,64,384]{4,2,1,0,3:T(4,128)(2,1)} %copy.134), calls=%async_computation.1 | async-start | bytes 2359296 | tf_op jit(solution)/shard_map/all_to_all | solution.py:75
  36.6 43.9 %all-to-all-start = ((bf16[3,2,4,64,384]{4,2,1,0,3:T(4,128)(2,1)}), bf16[3,2,4,64,384]{4,2,1,0,3:T(4,128)(2,1)}, u32[]{:S(2)}, u32[]{:S(2)}) async-start(bf16[3,2,4,64,384]{4,2,1,0,3:T(4,128)(2,1)} %copy.134), calls=%async_computation | async-start | bytes 2359296 | tf_op jit(solution)/shard_map/all_to_all | solution.py:65
  80.5 30.6 %all-to-all-start.2 = ((bf16[4,4,32,384]{3,2,1,0:T(8,128)(2,1)}), bf16[4,4,32,384]{3,2,1,0:T(8,128)(2,1)}, u32[]{:S(2)}, u32[]{:S(2)}) async-start(bf16[4,4,32,384]{3,2,1,0:T(8,128)(2,1)} %copy.167), calls=%async_computation.2 | async-start | bytes 786432 | tf_op jit(solution)/shard_map/all_to_all | solution.py:77
  84.7 60.3 %all-reduce.2.cloned.1.call-start = ((), (), s32[]{:S(2)}) async-start(), calls=%async_computation.4 | async-start | bytes 3145728 | tf_op jit(solution)/shard_map/psum | solution.py:83
  105.4 8.0 %collective-permute-start = (bf16[2,4,16,384]{3,2,1,0:T(8,128)(2,1)}, bf16[2,4,16,384]{3,2,1,0:T(8,128)(2,1)S(1)}, u32[]{:S(2)}, u32[]{:S(2)}) collective-permute-start(bf16[2,4,16,384]{3,2,1,0:T(8,128)(2,1)} %bitcast.113), channel_id=1, source_target_pairs={{0,4},{4,0},{8,12},{12,8},{1,5},{5,1},{9,13},{13,9},{2,6},{6,2},{1... | collective-permute-start | bytes 294920 | tf_op jit(solution)/shard_map/ppermute | solution.py:72
  108.1 8.6 %collective-permute-start.1 = (bf16[2,4,16,384]{3,2,1,0:T(8,128)(2,1)}, bf16[2,4,16,384]{3,2,1,0:T(8,128)(2,1)}, u32[]{:S(2)}, u32[]{:S(2)}) collective-permute-start(bf16[2,4,16,384]{3,2,1,0:T(8,128)(2,1)} %bitcast.112), channel_id=1, source_target_pairs={{0,8},{4,12},{8,0},{12,4},{1,9},{5,13},{9,1},{13,5},{2,10},{6,14},... | collective-permute-start | bytes 294920 | tf_op jit(solution)/shard_map/ppermute | solution.py:72
  111.1 6.8 %collective-permute-start.2 = (bf16[2,4,16,384]{3,2,1,0:T(8,128)(2,1)}, bf16[2,4,16,384]{3,2,1,0:T(8,128)(2,1)}, u32[]{:S(2)}, u32[]{:S(2)}) collective-permute-start(bf16[2,4,16,384]{3,2,1,0:T(8,128)(2,1)} %bitcast.111), channel_id=1, source_target_pairs={{0,12},{4,8},{8,4},{12,0},{1,13},{5,9},{9,5},{13,1},{2,14},{6,10},... | collective-permute-start | bytes 294920 | tf_op jit(solution)/shard_map/ppermute | solution.py:72
  124.5 52.1 %all-gather.3.cloned.1.call-start = ((), (), s32[]{:S(2)}) async-start(), calls=%async_computation.5 | async-start | bytes 2949120 | tf_op jit(solution)/shard_map/all_gather | solution.py:88
  125.1 101.7 %all-gather.5.cloned.1.call-start = ((), (), s32[]{:S(2)}) async-start(), calls=%async_computation.6 | async-start | bytes 2949120 | tf_op jit(solution)/shard_map/all_gather | solution.py:92
  125.7 101.1 %copy-start.4 = (f32[768]{0:T(1024)S(1)}, f32[768]{0:T(1024)}, u32[]{:S(2)}) copy-start(f32[768]{0:T(1024)} %param.11) | copy-start | bytes 9220
  125.7 120.8 %reduce-scatter.4.cloned.1.call-start = ((), (), s32[]{:S(2)}) async-start(), calls=%async_computation.7 | async-start | bytes 1179648
  146.6 1.2 copy-start.1
Sparse Core Ops, SparseCore 0:
  124.7 20.3 all-reduce.1
  239.6 6.8 reduce-scatter.3
Sparse Core Ops, SparseCore 1:
  126.7 49.9 all-gather.2
  178.1 48.6 all-gather.4
